TPU v7x, 256 devices: a whole 4x4x8 slice. The times are simulated.
256 devices in a mesh: lat: 4 (over y_lo, core), lon: 64 (over x, y_hi, z).
Axes of the slice: x: 4, y: 4 (y_hi: 2, y_lo: 2; y = y_hi * 2 + y_lo), z: 8, core: 2. Of those that a mesh axis runs over, the one named last changes fastest.
Arguments:
- inputs: bfloat16 [48, 1536, 2, 512], P('lat', 'lon'), may hold values from -6 to 6
- shift_lat: int32 [1], replicated, may hold values from 1 to 5
- shift_lon: int32 [1], replicated, may hold values from 1 to 11
- gain_attn: float32 [512], replicated, may hold values from 0.1 to 1.9
- w_qkv: bfloat16 [512, 1536], replicated, may hold values from -0.25 to 0.25
- w_out: bfloat16 [512, 512], replicated, may hold values from -0.25 to 0.25
- gain_merge: float32 [2048], replicated, may hold values from 0.1 to 1.9
- w_merge: bfloat16 [2048, 1024], replicated, may hold values from -0.125 to 0.125
- cot_coarse: bfloat16 [24, 768, 2, 1024], P('lat', 'lon'), may hold values from -6 to 6
- cot_skip: bfloat16 [48, 1536, 2, 512], P('lat', 'lon'), may hold values from -6 to 6
Outputs:
- coarse: bfloat16 [24, 768, 2, 1024], P('lat', 'lon')
- skip: bfloat16 [48, 1536, 2, 512], P('lat', 'lon')
- grad_input: bfloat16 [48, 1536, 2, 512], P('lat', 'lon')
All inputs are finite; a program needn't handle non-finite values.
Results may differ from a plain program's by a relative error of at most 0.015.
Values may be sent and summed in bfloat16 or wider, within the bound.
A program may use at most 128 MiB of HBM per device.

v0:
```python
import functools

import jax
import jax.numpy as jnp
from jax import lax
from jax.experimental import pallas as pl
from jax.experimental.pallas import tpu as pltpu
from jax.sharding import PartitionSpec as P

WLAT = 6
WLON = 12
PAIRS = 4
TOK = 144
FEAT = 512
EPS = 1e-05
BF = jnp.bfloat16
F32 = jnp.float32
MESH = pl.DeviceIdType.MESH
VMEM = 48 * 2**20
STRIPS = 3


def dot(a, b):
    return jnp.dot(a, b, preferred_element_type=F32)


def dot_t(a, b):
    return lax.dot_general(a, b, (((1,), (1,)), ((), ())), preferred_element_type=F32)


def t_dot(a, b):
    return lax.dot_general(a, b, (((0,), (0,)), ((), ())), preferred_element_type=F32)


def kernel(
    behind_lat, behind_lon, halo_lat, halo_lon,
    shift_lat, shift_lon, gain_attn_hbm, gain_merge_hbm,
    inputs, w_qkv_hbm, w_out_hbm, w_merge_hbm, cot_coarse_hbm, cot_skip_hbm,
    coarse_hbm, skip_hbm, grad_hbm,
    gain_attn, gain_merge,
    own, ext, bext, gext, rext, gskip, skip, cot_skip, cot_coarse, coarse, out,
    w_qkv, w_out, w_merge,
    gm, merged, token, norm, rstd, proj, mixed, soft, dproj, bias,
    local_sem, out_sem, send_sem, recv_sem,
):
    rows, cols = own.shape[0], own.shape[1]
    lat, lon = lax.axis_index("lat"), lax.axis_index("lon")
    nlat, nlon = lax.axis_size("lat"), lax.axis_size("lon")
    band = rows * nlat
    li, lj = int(behind_lat), int(behind_lon)

    def device(step_lat, step_lon):
        return (lax.rem(lat + step_lat + nlat, nlat), lax.rem(lon + step_lon + nlon, nlon))

    dlat, dlon = 1 - 2 * li, 1 - 2 * lj
    steps = ((dlat, 0), (0, dlon), (dlat, dlon))
    own_r, own_c = li * halo_lat, lj * halo_lon
    halo_r, halo_c = (1 - li) * rows, (1 - lj) * cols
    back_r, back_c = (1 - li) * halo_lat, (1 - lj) * halo_lon
    bhalo_r, bhalo_c = li * rows, lj * cols
    edge_r, edge_c = li * (rows - halo_lat), lj * (cols - halo_lon)
    bedge_r, bedge_c = (1 - li) * (rows - halo_lat), (1 - lj) * (cols - halo_lon)

    def send(phase, i, source, src, target, dst, step_lat, step_lon):
        (r, c, n, m), (tr, tc) = src, dst
        return pltpu.make_async_remote_copy(
            src_ref=source.at[pl.ds(r, n), pl.ds(c, m)],
            dst_ref=target.at[pl.ds(tr, n), pl.ds(tc, m)],
            send_sem=send_sem.at[phase, i],
            recv_sem=recv_sem.at[phase, i],
            device_id=device(step_lat, step_lon),
            device_id_type=MESH,
        )

    def ahead(phase, source, r, c, target):
        er, ec = r + edge_r, c + edge_c
        return (
            send(phase, 0, source, (er, c, halo_lat, cols), target, (halo_r, own_c), -dlat, 0),
            send(phase, 1, source, (r, ec, rows, halo_lon), target, (own_r, halo_c), 0, -dlon),
            send(phase, 2, source, (er, ec, halo_lat, halo_lon), target, (halo_r, halo_c), -dlat, -dlon),
        )

    def back(phase, ref):
        er, ec = back_r + bedge_r, back_c + bedge_c
        far_r, far_c = back_r + (1 - li) * WLAT, back_c + (1 - lj) * WLON
        near_r, near_c = back_r + li * WLAT, back_c + lj * WLON
        return (
            send(phase, 0, ref, (er, ec, halo_lat, halo_lon), ref, (bhalo_r, bhalo_c), dlat, dlon),
            send(phase, 1, ref, (far_r, ec, WLAT, halo_lon), ref, (far_r, bhalo_c), 0, dlon),
            send(phase, 2, ref, (er, far_c, halo_lat, WLON), ref, (bhalo_r, far_c), dlat, 0),
            send(phase, 3, ref, (near_r, ec, WLAT, halo_lon), ref, (near_r, bhalo_c), 0, dlon),
            send(phase, 4, ref, (er, near_c, halo_lat, WLON), ref, (bhalo_r, near_c), dlat, 0),
        )

    inner = (pl.ds(own_r, rows), pl.ds(own_c, cols))
    loads = [
        pltpu.make_async_copy(src, dst, local_sem.at[i])
        for i, (src, dst) in enumerate((
            (cot_coarse_hbm, cot_coarse),
            (w_merge_hbm, w_merge),
            (gain_attn_hbm, gain_attn),
            (inputs, own),
            (w_qkv_hbm, w_qkv),
            (w_out_hbm, w_out),
            (inputs, ext.at[inner]),
            (cot_skip_hbm, cot_skip),
            (gain_merge_hbm, gain_merge),
        ))
    ]
    barrier = pltpu.get_barrier_semaphore()
    for sr, sc in steps:
        pl.semaphore_signal(barrier, inc=1, device_id=device(sr, sc), device_id_type=MESH)
        pl.semaphore_signal(barrier, inc=1, device_id=device(-sr, -sc), device_id_type=MESH)
    for load in loads:
        load.start()
    pl.semaphore_wait(barrier, 6)
    first = ahead(0, inputs, 0, 0, ext)
    for copy in first:
        copy.start()
    second = back(1, bext)
    third = ahead(2, gext, own_r, own_c, gext)
    fourth = back(3, rext)

    s_lat, s_lon = shift_lat[0], shift_lon[0]
    t_lat = jnp.clip(s_lat - li * (WLAT - halo_lat), 0, halo_lat)
    t_lon = jnp.clip(s_lon - lj * (WLON - halo_lon), 0, halo_lon)

    low = lax.broadcasted_iota(jnp.int32, (TOK, 128), 1) < 64
    zero = jnp.zeros((TOK, 128), BF)

    def both(x):
        return jnp.concatenate([jnp.where(low, x, zero), jnp.where(low, zero, x)], 0)

    def unite(x):
        return jnp.where(low, x[:TOK], x[TOK:])

    start = lax.rem(rows * lat + WLAT * (1 - 2 * li) + band, band)
    edge = 2 * WLON * (band - s_lat - start)
    row_in = lax.broadcasted_iota(jnp.int32, (TOK, TOK), 0) >= edge
    col_in = lax.broadcasted_iota(jnp.int32, (TOK, TOK), 1) >= edge
    apart = jnp.where(row_in != col_in, F32(-1e30), F32(0.0))
    bias[0] = jnp.zeros((TOK, 2 * TOK), F32)
    bias[1] = jnp.concatenate([apart, apart], 1)

    def attend(i, across, p):
        at = p * 128
        q = both(proj[i, :, pl.ds(at, 128)] * BF(0.125))
        k = proj[i, :, pl.ds(FEAT + at, 128)]
        v = proj[i, :, pl.ds(2 * FEAT + at, 128)]
        scores = dot_t(k, q) + bias[across]
        e = jnp.exp(scores - jnp.max(scores, 0, keepdims=True))
        w = (e * (1.0 / jnp.sum(e, 0, keepdims=True))).astype(BF)
        soft[i, p] = w
        mixed[:, pl.ds(at, 128)] = unite(t_dot(w, v)).astype(BF)

    def attend_back(i, p):
        at = p * 128
        q = both(proj[i, :, pl.ds(at, 128)] * BF(0.125))
        k = proj[i, :, pl.ds(FEAT + at, 128)]
        v = proj[i, :, pl.ds(2 * FEAT + at, 128)]
        g = both(mixed[:, pl.ds(at, 128)])
        w = soft[i, p]
        dw = dot_t(v, g)
        wf = w.astype(F32)
        ds = (wf * (dw - jnp.sum(dw * wf, 0, keepdims=True))).astype(BF)
        dproj[:, pl.ds(at, 128)] = (unite(t_dot(ds, k)) * 0.125).astype(BF)
        dproj[:, pl.ds(FEAT + at, 128)] = dot(ds, q).astype(BF)
        dproj[:, pl.ds(2 * FEAT + at, 128)] = dot(w, g).astype(BF)

    def windows(forward, ready, local_ref, wide_ref, result_ref, copies):
        def step(i, carry):
            across_lat, across_lon = i % 2, ((i + 1) // 2) % 2
            wr = WLAT * (li + dlat * across_lat)
            wc = WLON * (lj + dlon * across_lon)

            @pl.when(i == 0)
            def _():
                x = local_ref[pl.ds(s_lat, WLAT), pl.ds(s_lon, WLON)]
                token[...] = x.reshape(TOK, FEAT)

            @pl.when(i == 1)
            def _():
                for copy in ready:
                    copy.wait_recv()

            @pl.when(i > 0)
            def _():
                x = wide_ref[pl.ds(t_lat + wr, WLAT), pl.ds(t_lon + wc, WLON)]
                token[...] = x.reshape(TOK, FEAT)

            if forward:
                x = token[...].astype(F32)
                mean = jnp.mean(x, -1, keepdims=True)
                x = x - mean
                inv = lax.rsqrt(jnp.mean(x * x, -1, keepdims=True) + EPS)
                x = x * inv
                norm[i] = x
                rstd[i] = jnp.broadcast_to(inv, (TOK, 128))
                proj[i] = dot((x * gain_attn[...]).astype(BF), w_qkv[...]).astype(BF)
                for p in range(PAIRS):
                    attend(i, across_lat, p)
                result = dot(mixed[...], w_out[...]).astype(BF)
            else:
                mixed[...] = dot_t(token[...], w_out[...]).astype(BF)
                for p in range(PAIRS):
                    attend_back(i, p)
                d = dot_t(dproj[...], w_qkv[...]).astype(BF).astype(F32) * gain_attn[...]
                nn = norm[i]
                inv = rstd[i][:, :1]
                result = (inv * (
                    d - jnp.mean(d, -1, keepdims=True) - nn * jnp.mean(d * nn, -1, keepdims=True)
                )).astype(BF)
            result_ref[pl.ds(back_r + wr, WLAT), pl.ds(back_c + wc, WLON)] = result.reshape(
                WLAT, WLON, 2, FEAT
            )
            for turn, part in ((1, copies[:3]), (2, copies[3:4]), (3, copies[4:])):
                @pl.when(i == turn)
                def _(part=part):
                    for copy in part:
                        copy.start()
            return carry

        lax.fori_loop(0, 4, step, 0)

    loads[0].wait()
    loads[1].wait()
    strip = TOK // STRIPS

    def quarter_back(j, carry):
        at = pl.multiple_of(j * FEAT, FEAT)
        x = cot_coarse.reshape(TOK, 2 * FEAT)[...]
        y = dot_t(x, w_merge[pl.ds(at, FEAT), :]).astype(BF)
        gm[:, :, pl.ds(at, FEAT)] = y.reshape(STRIPS, strip, FEAT)
        return carry

    lax.fori_loop(0, 4, quarter_back, 0)
    for load in loads[2:7]:
        load.wait()
    windows(True, first, own, ext, bext, second)
    loads[7].wait()
    loads[8].wait()
    for copy in second:
        copy.wait_recv()

    start_r, start_c = halo_lat - t_lat, halo_lon - t_lon
    high = rows // STRIPS
    width = 4 * FEAT
    patches = (rows // 2, 2, cols // 2, 2, 2, FEAT)
    quarters = [(a, b) for a in range(2) for b in range(2)]

    def merge(turn, carry):
        j = (STRIPS - 1 - turn) if li else turn
        mine = pl.ds(high * j, high)
        skip[mine] = (
            own[mine].astype(F32)
            + bext[pl.ds(start_r + high * j, high), pl.ds(start_c, cols)].astype(F32)
        ).astype(BF)

        def quarter(ref, a, b):
            return ref.reshape(*patches)[pl.ds(high // 2 * j, high // 2), a, :, b].reshape(strip, FEAT)

        parts = [quarter(skip, a, b).astype(F32) for a, b in quarters]
        mean = sum(jnp.sum(x, -1, keepdims=True) for x in parts) / width
        parts = [x - mean for x in parts]
        inv = lax.rsqrt(sum(jnp.sum(x * x, -1, keepdims=True) for x in parts) / width + EPS)
        parts = [x * inv for x in parts]
        grads = []
        for i, x in enumerate(parts):
            gain = gain_merge[:, pl.ds(i * FEAT, FEAT)]
            merged[j, :, pl.ds(i * FEAT, FEAT)] = (x * gain).astype(BF)
            grads.append(gm[j, :, pl.ds(i * FEAT, FEAT)].astype(F32) * gain)
        mean_g = sum(jnp.sum(g, -1, keepdims=True) for g in grads) / width
        mean_gx = sum(jnp.sum(g * x, -1, keepdims=True) for g, x in zip(grads, parts)) / width
        for (a, b), g, x in zip(quarters, grads, parts):
            d = (inv * (g - mean_g - x * mean_gx)).astype(BF) + quarter(cot_skip, a, b)
            gskip.reshape(*patches)[pl.ds(high // 2 * j, high // 2), a, :, b] = d.reshape(
                high // 2, cols // 2, 2, FEAT
            )
        gext[pl.ds(own_r + high * j, high), pl.ds(own_c, cols)] = gskip[mine]

        @pl.when(turn == 0)
        def _():
            third[0].start()
            third[2].start()

        return carry

    lax.fori_loop(0, STRIPS, merge, 0)
    third[1].start()
    skip_out = pltpu.make_async_copy(skip, skip_hbm, out_sem.at[0])
    skip_out.start()
    windows(False, third, gskip, gext, rext, fourth)

    def coarse_part(j, carry):
        at = pl.multiple_of(j * FEAT, FEAT)
        x = merged.reshape(TOK, width)[...]
        coarse.reshape(TOK, 2 * FEAT)[:, pl.ds(at, FEAT)] = dot(
            x, w_merge[:, pl.ds(at, FEAT)]
        ).astype(BF)
        return carry

    lax.fori_loop(0, 2, coarse_part, 0)
    coarse_out = pltpu.make_async_copy(coarse, coarse_hbm, out_sem.at[1])
    coarse_out.start()
    for copy in fourth:
        copy.wait_recv()

    def finish(j, carry):
        mine = pl.ds(high * j, high)
        out[mine] = gskip[mine] + rext[pl.ds(start_r + high * j, high), pl.ds(start_c, cols)]
        return carry

    lax.fori_loop(0, STRIPS, finish, 0)
    grad_out = pltpu.make_async_copy(out, grad_hbm, out_sem.at[2])
    grad_out.start()
    for copy in first + second + third + fourth:
        copy.wait_send()
    skip_out.wait()
    coarse_out.wait()
    grad_out.wait()


def block(behind_lat, behind_lon, halo_lat, halo_lon, ident, args):
    (inputs, shift_lat, shift_lon, gain_attn, w_qkv, w_out, gain_merge, w_merge,
     cot_coarse, cot_skip) = args
    rows, cols, lev, feat = inputs.shape
    wide = (rows + halo_lat, cols + halo_lon, lev, feat)
    smem = pl.BlockSpec(memory_space=pltpu.SMEM)
    hbm = pl.BlockSpec(memory_space=pltpu.HBM)
    anyw = pl.BlockSpec(memory_space=pl.ANY)
    tile, coarse = pltpu.VMEM(inputs.shape, BF), pltpu.VMEM(cot_coarse.shape, BF)
    return pl.pallas_call(
        functools.partial(kernel, behind_lat, behind_lon, halo_lat, halo_lon),
        out_shape=(
            jax.ShapeDtypeStruct(cot_coarse.shape, BF),
            jax.ShapeDtypeStruct(inputs.shape, BF),
            jax.ShapeDtypeStruct(inputs.shape, BF),
        ),
        in_specs=[smem, smem] + [hbm] * 8,
        out_specs=(anyw, anyw, anyw),
        scratch_shapes=[
            pltpu.VMEM((1, feat), F32),
            pltpu.VMEM((1, 4 * feat), F32),
            tile,
            pltpu.VMEM(wide, BF),
            pltpu.VMEM(wide, BF),
            pltpu.VMEM(wide, BF),
            pltpu.VMEM(wide, BF),
            tile, tile, tile, coarse, coarse, tile,
            pltpu.VMEM(w_qkv.shape, BF),
            pltpu.VMEM(w_out.shape, BF),
            pltpu.VMEM(w_merge.shape, BF),
            pltpu.VMEM((STRIPS, TOK // STRIPS, 4 * FEAT), BF),
            pltpu.VMEM((STRIPS, TOK // STRIPS, 4 * FEAT), BF),
            pltpu.VMEM((TOK, FEAT), BF),
            pltpu.VMEM((4, TOK, FEAT), F32),
            pltpu.VMEM((4, TOK, 128), F32),
            pltpu.VMEM((4, TOK, 3 * FEAT), BF),
            pltpu.VMEM((TOK, FEAT), BF),
            pltpu.VMEM((4, PAIRS, TOK, 2 * TOK), BF),
            pltpu.VMEM((TOK, 3 * FEAT), BF),
            pltpu.VMEM((2, TOK, 2 * TOK), F32),
            pltpu.SemaphoreType.DMA((9,)),
            pltpu.SemaphoreType.DMA((3,)),
            pltpu.SemaphoreType.DMA((4, 5)),
            pltpu.SemaphoreType.DMA((4, 5)),
        ],
        compiler_params=pltpu.CompilerParams(
            collective_id=ident, has_side_effects=True, vmem_limit_bytes=VMEM
        ),
    )(
        shift_lat, shift_lon, gain_attn.reshape(1, -1), gain_merge.reshape(1, -1),
        inputs, w_qkv, w_out, w_merge, cot_coarse, cot_skip,
    )


def local(*args):
    half_lat, half_lon = WLAT // 2, WLON // 2
    behind_lat = (args[1][0] > half_lat).astype(jnp.int32)
    behind_lon = (args[2][0] > half_lon).astype(jnp.int32)
    return lax.switch(
        2 * behind_lat + behind_lon,
        [
            functools.partial(block, bool(i // 2), bool(i % 2), half_lat, half_lon, i)
            for i in range(4)
        ],
        args,
    )


def solution(mesh):
    tile = P("lat", "lon", None, None)
    return jax.shard_map(
        local,
        mesh=mesh,
        in_specs=(tile, P(), P(), P(), P(), P(), P(), P(), tile, tile),
        out_specs=(tile, tile, tile),
        check_vma=False,
    )
```

profile of v0, /device:TPU:1, one launch (start us, length us, event | category | flops | bytes accessed | tf_op | source)
XLA Modules:
  0.0 56.8 jit_solution(14862696612490154444)
XLA Ops:
  1.9 52.5 %conditional.1 = ((bf16[6,12,2,1024]{3,2,1,0:T(2,128)(2,1)S(1)}, bf16[12,24,2,512]{3,2,1,0:T(2,128)(2,1)S(1)}, bf16[12,24,2,512]{3,2,1,0:T(2,128)(2,1)S(1)})) conditional(s32[]{:T(128)} %bitcast.8, (f32[512]{0:T(512)}, f32[2048]{0:T(1024)}, s32[1]{0:T(128)}, s32[1]{0:T(128)}, bf16[12,24,2,512]{3,2,1,0:T(2,128)(2,1)}, ...), branch_computations={%region_0.0_spmd, %region_1.0_spmd, %region_2.0_spmd, %region_3.0_... | conditional | bytes 8 | solution.py:381
  1.9 52.3 %branch_0_fun.1 = (bf16[6,12,2,1024]{3,2,1,0:T(2,128)(2,1)S(1)}, bf16[12,24,2,512]{3,2,1,0:T(2,128)(2,1)S(1)}, bf16[12,24,2,512]{3,2,1,0:T(2,128)(2,1)S(1)}) custom-call(s32[1]{0:T(128)} %get-tuple-element.80.shift_lat, s32[1]{0:T(128)} %get-tuple-element.81.shift_lon, f32[1,512]{1,0:T(1,128)} %bitcast.13, f32[1,2048]{1,0:T(1,128)} %bitcast.9, ...), custom_call_target="tpu_custom_call" | custom-call | tf_op jit(solution)/shard_map/cond/branch_0_fun/pallas_call | solution.py:332
  54.5 0.7 %copy.42 = bf16[6,12,2,1024]{3,2,1,0:T(2,128)(2,1)} copy(bf16[6,12,2,1024]{3,2,1,0:T(2,128)(2,1)S(1)} %get-tuple-element.153) | data formatting | bytes 589824
  55.2 0.8 %copy.43 = bf16[12,24,2,512]{3,2,1,0:T(2,128)(2,1)} copy(bf16[12,24,2,512]{3,2,1,0:T(2,128)(2,1)S(1)} %get-tuple-element.154) | data formatting | bytes 1179648
  56.0 0.8 %copy.44 = bf16[12,24,2,512]{3,2,1,0:T(2,128)(2,1)} copy(bf16[12,24,2,512]{3,2,1,0:T(2,128)(2,1)S(1)} %get-tuple-element.155) | data formatting | bytes 1179648
where the time goes:
time: 57.2 us; the launch traced here: 56.8 us
  Pallas kernels  52.3 us (91%)
  local copies, waits for them, and re-layouts  2.34 us (4%)
  between operations  1.94 us (3%)
    pallas_call x1, Pallas kernels, block(): pl.pallas_call(functools.partial(kernel, behind_lat, behind_lon, halo_lat...  52.3 us
    unnamed x3, local copies, waits for them, and re-layouts  2.34 us

commit v1 on v0

--- a/solution.py
+++ b/solution.py
@@ -38,7 +38,7 @@
     inputs, w_qkv_hbm, w_out_hbm, w_merge_hbm, cot_coarse_hbm, cot_skip_hbm,
     coarse_hbm, skip_hbm, grad_hbm,
     gain_attn, gain_merge,
-    own, ext, bext, gext, rext, gskip, skip, cot_skip, cot_coarse, coarse, out,
+    own, xtall, btall, gtall, ext, bext, gext, rext, gskip, skip, cot_skip, cot_coarse, coarse, out,
     w_qkv, w_out, w_merge,
     gm, merged, token, norm, rstd, proj, mixed, soft, dproj, bias,
     local_sem, out_sem, send_sem, recv_sem,
@@ -72,24 +72,24 @@
             device_id_type=MESH,
         )
 
-    def ahead(phase, source, r, c, target):
+    def ahead(phase, source, r, c, tall, wide):
         er, ec = r + edge_r, c + edge_c
         return (
-            send(phase, 0, source, (er, c, halo_lat, cols), target, (halo_r, own_c), -dlat, 0),
-            send(phase, 1, source, (r, ec, rows, halo_lon), target, (own_r, halo_c), 0, -dlon),
-            send(phase, 2, source, (er, ec, halo_lat, halo_lon), target, (halo_r, halo_c), -dlat, -dlon),
+            send(phase, 0, source, (er, c, halo_lat, cols), tall, (halo_r, 0), -dlat, 0),
+            send(phase, 1, source, (r, ec, rows, halo_lon), wide, (own_r, halo_c), 0, -dlon),
+            send(phase, 2, source, (er, ec, halo_lat, halo_lon), wide, (halo_r, halo_c), -dlat, -dlon),
         )
 
-    def back(phase, ref):
+    def back(phase, tall, at_c, wide):
         er, ec = back_r + bedge_r, back_c + bedge_c
-        far_r, far_c = back_r + (1 - li) * WLAT, back_c + (1 - lj) * WLON
-        near_r, near_c = back_r + li * WLAT, back_c + lj * WLON
+        far_r, near_r = back_r + (1 - li) * WLAT, back_r + li * WLAT
+        far_c, near_c = at_c + (1 - lj) * WLON, at_c + lj * WLON
         return (
-            send(phase, 0, ref, (er, ec, halo_lat, halo_lon), ref, (bhalo_r, bhalo_c), dlat, dlon),
-            send(phase, 1, ref, (far_r, ec, WLAT, halo_lon), ref, (far_r, bhalo_c), 0, dlon),
-            send(phase, 2, ref, (er, far_c, halo_lat, WLON), ref, (bhalo_r, far_c), dlat, 0),
-            send(phase, 3, ref, (near_r, ec, WLAT, halo_lon), ref, (near_r, bhalo_c), 0, dlon),
-            send(phase, 4, ref, (er, near_c, halo_lat, WLON), ref, (bhalo_r, near_c), dlat, 0),
+            send(phase, 0, tall, (er, near_c, halo_lat, WLON), tall, (bhalo_r, near_c), dlat, 0),
+            send(phase, 1, wide, (er, ec, halo_lat, halo_lon), wide, (bhalo_r, bhalo_c), dlat, dlon),
+            send(phase, 2, wide, (far_r, ec, WLAT, halo_lon), wide, (far_r, bhalo_c), 0, dlon),
+            send(phase, 3, tall, (er, far_c, halo_lat, WLON), tall, (bhalo_r, far_c), dlat, 0),
+            send(phase, 4, wide, (near_r, ec, WLAT, halo_lon), wide, (near_r, bhalo_c), 0, dlon),
         )
 
     inner = (pl.ds(own_r, rows), pl.ds(own_c, cols))
@@ -102,6 +102,7 @@
             (inputs, own),
             (w_qkv_hbm, w_qkv),
             (w_out_hbm, w_out),
+            (inputs, xtall.at[pl.ds(own_r, rows)]),
             (inputs, ext.at[inner]),
             (cot_skip_hbm, cot_skip),
             (gain_merge_hbm, gain_merge),
@@ -114,12 +115,12 @@
     for load in loads:
         load.start()
     pl.semaphore_wait(barrier, 6)
-    first = ahead(0, inputs, 0, 0, ext)
-    for copy in first:
-        copy.start()
-    second = back(1, bext)
-    third = ahead(2, gext, own_r, own_c, gext)
-    fourth = back(3, rext)
+    first = ahead(0, inputs, 0, 0, xtall, ext)
+    for turn in (1, 2, 0):
+        first[turn].start()
+    second = back(1, btall, 0, bext)
+    third = ahead(2, gskip, 0, 0, gtall, gext)
+    fourth = back(3, rext, back_c, rext)
 
     s_lat, s_lon = shift_lat[0], shift_lon[0]
     t_lat = jnp.clip(s_lat - li * (WLAT - halo_lat), 0, halo_lat)
@@ -167,9 +168,9 @@
         dproj[:, pl.ds(FEAT + at, 128)] = dot(ds, q).astype(BF)
         dproj[:, pl.ds(2 * FEAT + at, 128)] = dot(w, g).astype(BF)
 
-    def windows(forward, ready, local_ref, wide_ref, result_ref, copies):
+    def windows(forward, ready, local_ref, tall, wide, results, copies):
         def step(i, carry):
-            across_lat, across_lon = i % 2, ((i + 1) // 2) % 2
+            across_lat, across_lon = ((i + 1) // 2) % 2, i // 2
             wr = WLAT * (li + dlat * across_lat)
             wc = WLON * (lj + dlon * across_lon)
 
@@ -180,12 +181,19 @@
 
             @pl.when(i == 1)
             def _():
-                for copy in ready:
-                    copy.wait_recv()
-
-            @pl.when(i > 0)
+                ready[0].wait_recv()
+                x = tall[pl.ds(t_lat + wr, WLAT), pl.ds(s_lon, WLON)]
+                token[...] = x.reshape(TOK, FEAT)
+
+            @pl.when(i == 2)
             def _():
-                x = wide_ref[pl.ds(t_lat + wr, WLAT), pl.ds(t_lon + wc, WLON)]
+                ready[1].wait_recv()
+                ready[2].wait_recv()
+                wide[pl.ds(halo_r, halo_lat), pl.ds(own_c, cols)] = tall[pl.ds(halo_r, halo_lat)]
+
+            @pl.when(i >= 2)
+            def _():
+                x = wide[pl.ds(t_lat + wr, WLAT), pl.ds(t_lon + wc, WLON)]
                 token[...] = x.reshape(TOK, FEAT)
 
             if forward:
@@ -210,10 +218,10 @@
                 result = (inv * (
                     d - jnp.mean(d, -1, keepdims=True) - nn * jnp.mean(d * nn, -1, keepdims=True)
                 )).astype(BF)
-            result_ref[pl.ds(back_r + wr, WLAT), pl.ds(back_c + wc, WLON)] = result.reshape(
-                WLAT, WLON, 2, FEAT
-            )
-            for turn, part in ((1, copies[:3]), (2, copies[3:4]), (3, copies[4:])):
+            result = result.reshape(WLAT, WLON, 2, FEAT)
+            for ref, at_c in results:
+                ref[pl.ds(back_r + wr, WLAT), pl.ds(at_c + wc, WLON)] = result
+            for turn, part in ((1, copies[:1]), (2, copies[1:4]), (3, copies[4:])):
                 @pl.when(i == turn)
                 def _(part=part):
                     for copy in part:
@@ -224,40 +232,51 @@
 
     loads[0].wait()
     loads[1].wait()
-    strip = TOK // STRIPS
+    strip, slim = TOK // STRIPS, cols // STRIPS
+    thin = slim // 2
 
     def quarter_back(j, carry):
         at = pl.multiple_of(j * FEAT, FEAT)
-        x = cot_coarse.reshape(TOK, 2 * FEAT)[...]
+        x = jnp.concatenate(
+            [cot_coarse[:, k * thin:(k + 1) * thin].reshape(strip, 2 * FEAT) for k in range(STRIPS)], 0
+        )
         y = dot_t(x, w_merge[pl.ds(at, FEAT), :]).astype(BF)
         gm[:, :, pl.ds(at, FEAT)] = y.reshape(STRIPS, strip, FEAT)
         return carry
 
     lax.fori_loop(0, 4, quarter_back, 0)
-    for load in loads[2:7]:
+    for load in loads[2:8]:
         load.wait()
-    windows(True, first, own, ext, bext, second)
-    loads[7].wait()
+    windows(True, first, own, xtall, ext, ((btall, 0), (bext, back_c)), second)
     loads[8].wait()
-    for copy in second:
-        copy.wait_recv()
+    loads[9].wait()
+    second[0].wait_recv()
+    second[3].wait_recv()
 
     start_r, start_c = halo_lat - t_lat, halo_lon - t_lon
-    high = rows // STRIPS
     width = 4 * FEAT
     patches = (rows // 2, 2, cols // 2, 2, 2, FEAT)
     quarters = [(a, b) for a in range(2) for b in range(2)]
 
     def merge(turn, carry):
-        j = (STRIPS - 1 - turn) if li else turn
-        mine = pl.ds(high * j, high)
-        skip[mine] = (
-            own[mine].astype(F32)
-            + bext[pl.ds(start_r + high * j, high), pl.ds(start_c, cols)].astype(F32)
-        ).astype(BF)
+        j = turn if lj else lax.rem(turn + 1, STRIPS)
+        mine = pl.ds(slim * j, slim)
+
+        @pl.when(turn < STRIPS - 1)
+        def _():
+            placed = btall[pl.ds(start_r, rows), pl.ds(start_c - back_c + slim * j, slim)]
+            skip[:, mine] = (own[:, mine].astype(F32) + placed.astype(F32)).astype(BF)
+
+        @pl.when(turn == STRIPS - 1)
+        def _():
+            for i in (1, 2, 4):
+                second[i].wait_recv()
+            bext[pl.ds(bhalo_r, halo_lat), pl.ds(back_c, cols)] = btall[pl.ds(bhalo_r, halo_lat)]
+            placed = bext[pl.ds(start_r, rows), pl.ds(start_c + slim * j, slim)]
+            skip[:, mine] = (own[:, mine].astype(F32) + placed.astype(F32)).astype(BF)
 
         def quarter(ref, a, b):
-            return ref.reshape(*patches)[pl.ds(high // 2 * j, high // 2), a, :, b].reshape(strip, FEAT)
+            return ref.reshape(*patches)[:, a, pl.ds(thin * j, thin), b].reshape(strip, FEAT)
 
         parts = [quarter(skip, a, b).astype(F32) for a, b in quarters]
         mean = sum(jnp.sum(x, -1, keepdims=True) for x in parts) / width
@@ -273,30 +292,28 @@
         mean_gx = sum(jnp.sum(g * x, -1, keepdims=True) for g, x in zip(grads, parts)) / width
         for (a, b), g, x in zip(quarters, grads, parts):
             d = (inv * (g - mean_g - x * mean_gx)).astype(BF) + quarter(cot_skip, a, b)
-            gskip.reshape(*patches)[pl.ds(high // 2 * j, high // 2), a, :, b] = d.reshape(
-                high // 2, cols // 2, 2, FEAT
+            gskip.reshape(*patches)[:, a, pl.ds(thin * j, thin), b] = d.reshape(
+                rows // 2, thin, 2, FEAT
             )
-        gext[pl.ds(own_r + high * j, high), pl.ds(own_c, cols)] = gskip[mine]
-
-        @pl.when(turn == 0)
-        def _():
-            third[0].start()
-            third[2].start()
-
         return carry
 
     lax.fori_loop(0, STRIPS, merge, 0)
-    third[1].start()
+    for turn in (1, 2, 0):
+        third[turn].start()
+    gtall[pl.ds(own_r, rows)] = gskip[...]
+    gext[inner] = gskip[...]
     skip_out = pltpu.make_async_copy(skip, skip_hbm, out_sem.at[0])
     skip_out.start()
-    windows(False, third, gskip, gext, rext, fourth)
+    windows(False, third, gskip, gtall, gext, ((rext, back_c),), fourth)
 
     def coarse_part(j, carry):
         at = pl.multiple_of(j * FEAT, FEAT)
         x = merged.reshape(TOK, width)[...]
-        coarse.reshape(TOK, 2 * FEAT)[:, pl.ds(at, FEAT)] = dot(
-            x, w_merge[:, pl.ds(at, FEAT)]
-        ).astype(BF)
+        y = dot(x, w_merge[:, pl.ds(at, FEAT)]).astype(BF)
+        for k in range(STRIPS):
+            coarse[:, k * thin:(k + 1) * thin, :, pl.ds(at, FEAT)] = y[
+                k * strip:(k + 1) * strip
+            ].reshape(rows // 2, thin, 2, FEAT)
         return carry
 
     lax.fori_loop(0, 2, coarse_part, 0)
@@ -306,11 +323,11 @@
         copy.wait_recv()
 
     def finish(j, carry):
-        mine = pl.ds(high * j, high)
-        out[mine] = gskip[mine] + rext[pl.ds(start_r + high * j, high), pl.ds(start_c, cols)]
+        mine = pl.ds(4 * j, 4)
+        out[mine] = gskip[mine] + rext[pl.ds(start_r + 4 * j, 4), pl.ds(start_c, cols)]
         return carry
 
-    lax.fori_loop(0, STRIPS, finish, 0)
+    lax.fori_loop(0, rows // 4, finish, 0)
     grad_out = pltpu.make_async_copy(out, grad_hbm, out_sem.at[2])
     grad_out.start()
     for copy in first + second + third + fourth:
@@ -329,6 +346,7 @@
     hbm = pl.BlockSpec(memory_space=pltpu.HBM)
     anyw = pl.BlockSpec(memory_space=pl.ANY)
     tile, coarse = pltpu.VMEM(inputs.shape, BF), pltpu.VMEM(cot_coarse.shape, BF)
+    tall = pltpu.VMEM((rows + halo_lat, cols, lev, feat), BF)
     return pl.pallas_call(
         functools.partial(kernel, behind_lat, behind_lon, halo_lat, halo_lon),
         out_shape=(
@@ -342,6 +360,7 @@
             pltpu.VMEM((1, feat), F32),
             pltpu.VMEM((1, 4 * feat), F32),
             tile,
+            tall, tall, tall,
             pltpu.VMEM(wide, BF),
             pltpu.VMEM(wide, BF),
             pltpu.VMEM(wide, BF),
@@ -360,7 +379,7 @@
             pltpu.VMEM((4, PAIRS, TOK, 2 * TOK), BF),
             pltpu.VMEM((TOK, 3 * FEAT), BF),
             pltpu.VMEM((2, TOK, 2 * TOK), F32),
-            pltpu.SemaphoreType.DMA((9,)),
+            pltpu.SemaphoreType.DMA((10,)),
             pltpu.SemaphoreType.DMA((3,)),
             pltpu.SemaphoreType.DMA((4, 5)),
             pltpu.SemaphoreType.DMA((4, 5)),
@@ -374,11 +393,33 @@
     )
 
 
+def deliver(coarse, skip, grad, coarse_hbm, skip_hbm, grad_hbm, sem):
+    copies = [
+        pltpu.make_async_copy(src, dst, sem.at[i])
+        for i, (src, dst) in enumerate(((coarse, coarse_hbm), (skip, skip_hbm), (grad, grad_hbm)))
+    ]
+    for copy in copies:
+        copy.start()
+    for copy in copies:
+        copy.wait()
+
+
+def hand_out(results):
+    anyw = pl.BlockSpec(memory_space=pl.ANY)
+    return pl.pallas_call(
+        deliver,
+        out_shape=tuple(jax.ShapeDtypeStruct(x.shape, x.dtype) for x in results),
+        in_specs=[anyw] * 3,
+        out_specs=(pl.BlockSpec(memory_space=pltpu.HBM),) * 3,
+        scratch_shapes=[pltpu.SemaphoreType.DMA((3,))],
+    )(*results)
+
+
 def local(*args):
     half_lat, half_lon = WLAT // 2, WLON // 2
     behind_lat = (args[1][0] > half_lat).astype(jnp.int32)
     behind_lon = (args[2][0] > half_lon).astype(jnp.int32)
-    return lax.switch(
+    results = lax.switch(
         2 * behind_lat + behind_lon,
         [
             functools.partial(block, bool(i // 2), bool(i % 2), half_lat, half_lon, i)
@@ -386,6 +427,7 @@
         ],
         args,
     )
+    return hand_out(results)
 
 
 def solution(mesh):

time: 57.2 us -> 56.2 us (0.983)
  local copies, waits for them, and re-layouts: 2.34 us -> 0 us
  Pallas kernels: 52.3 us -> 53.7 us
    unnamed x3 -> x0, local copies, waits for them, and re-layouts: 2.34 us -> none
    pallas_call x0 -> x1, Pallas kernels: none -> 1.13 us  [hand_out(): pl.pallas_call(deliver, out_shape=tuple((jax.ShapeDtypeStruct(x.shape, x....]
where the time goes in v1:
time: 56.2 us; the launch traced here: 56.1 us
  Pallas kernels  53.7 us (96%)
  between operations  2.12 us (4%)
    pallas_call x1, Pallas kernels, block(): pl.pallas_call(functools.partial(kernel, behind_lat, behind_lon, halo_lat...  52.6 us
    pallas_call x1, Pallas kernels, hand_out(): pl.pallas_call(deliver, out_shape=tuple((jax.ShapeDtypeStruct(x.shape, x....  1.13 us

profile of v1, /device:TPU:1, one launch (start us, length us, event | category | flops | bytes accessed | tf_op | source)
XLA Modules:
  0.0 56.1 jit_solution(1280512606598049614)
XLA Ops:
  1.9 52.9 %conditional.1 = ((bf16[6,12,2,1024]{3,2,1,0:T(2,128)(2,1)S(1)}, bf16[12,24,2,512]{3,2,1,0:T(2,128)(2,1)S(1)}, bf16[12,24,2,512]{3,2,1,0:T(2,128)(2,1)S(1)})) conditional(s32[]{:T(128)} %bitcast.8, (f32[512]{0:T(512)}, f32[2048]{0:T(1024)}, s32[1]{0:T(128)}, s32[1]{0:T(128)}, bf16[12,24,2,512]{3,2,1,0:T(2,128)(2,1)}, ...), branch_computations={%region_0.0_spmd, %region_1.0_spmd, %region_2.0_spmd, %region_3.0_... | conditional | bytes 8 | solution.py:422
  1.9 52.6 %branch_0_fun.1 = (bf16[6,12,2,1024]{3,2,1,0:T(2,128)(2,1)S(1)}, bf16[12,24,2,512]{3,2,1,0:T(2,128)(2,1)S(1)}, bf16[12,24,2,512]{3,2,1,0:T(2,128)(2,1)S(1)}) custom-call(s32[1]{0:T(128)} %get-tuple-element.80.shift_lat, s32[1]{0:T(128)} %get-tuple-element.81.shift_lon, f32[1,512]{1,0:T(1,128)} %bitcast.13, f32[1,2048]{1,0:T(1,128)} %bitcast.9, ...), custom_call_target="tpu_custom_call" | custom-call | tf_op jit(solution)/shard_map/cond/branch_0_fun/pallas_call | solution.py:350
  54.8 1.1 %shard_map.121 = (bf16[6,12,2,1024]{3,2,1,0:T(2,128)(2,1)}, bf16[12,24,2,512]{3,2,1,0:T(2,128)(2,1)}, bf16[12,24,2,512]{3,2,1,0:T(2,128)(2,1)}) custom-call(bf16[6,12,2,1024]{3,2,1,0:T(2,128)(2,1)S(1)} %get-tuple-element.126.coarse, bf16[12,24,2,512]{3,2,1,0:T(2,128)(2,1)S(1)} %get-tuple-element.127.skip, bf16[12,24,2,512]{3,2,1,0:T(2,128)(2,1)S(1)} %get-tuple-element.128.grad), custom_call_target="tpu_custom_call" | custom-call | tf_op jit(solution)/shard_map/pallas_call | solution.py:409

commit v2 on v1

--- a/solution.py
+++ b/solution.py
@@ -12,6 +12,7 @@
 PAIRS = 4
 TOK = 144
 FEAT = 512
+HALF = FEAT // 2
 EPS = 1e-05
 BF = jnp.bfloat16
 F32 = jnp.float32
@@ -38,7 +39,7 @@
     inputs, w_qkv_hbm, w_out_hbm, w_merge_hbm, cot_coarse_hbm, cot_skip_hbm,
     coarse_hbm, skip_hbm, grad_hbm,
     gain_attn, gain_merge,
-    own, xtall, btall, gtall, ext, bext, gext, rext, gskip, skip, cot_skip, cot_coarse, coarse, out,
+    own, xtall, btall, gtall, rtall, ext, bext, gext, rext, gskip, skip, cot_skip, cot_coarse, coarse, out,
     w_qkv, w_out, w_merge,
     gm, merged, token, norm, rstd, proj, mixed, soft, dproj, bias,
     local_sem, out_sem, send_sem, recv_sem,
@@ -80,16 +81,14 @@
             send(phase, 2, source, (er, ec, halo_lat, halo_lon), wide, (halo_r, halo_c), -dlat, -dlon),
         )
 
-    def back(phase, tall, at_c, wide):
+    def back(phase, tall, wide):
         er, ec = back_r + bedge_r, back_c + bedge_c
-        far_r, near_r = back_r + (1 - li) * WLAT, back_r + li * WLAT
-        far_c, near_c = at_c + (1 - lj) * WLON, at_c + lj * WLON
+        near_c, far_c = lj * WLON, (1 - lj) * WLON
         return (
             send(phase, 0, tall, (er, near_c, halo_lat, WLON), tall, (bhalo_r, near_c), dlat, 0),
             send(phase, 1, wide, (er, ec, halo_lat, halo_lon), wide, (bhalo_r, bhalo_c), dlat, dlon),
-            send(phase, 2, wide, (far_r, ec, WLAT, halo_lon), wide, (far_r, bhalo_c), 0, dlon),
+            send(phase, 2, wide, (back_r, ec, rows, halo_lon), wide, (back_r, bhalo_c), 0, dlon),
             send(phase, 3, tall, (er, far_c, halo_lat, WLON), tall, (bhalo_r, far_c), dlat, 0),
-            send(phase, 4, wide, (near_r, ec, WLAT, halo_lon), wide, (near_r, bhalo_c), 0, dlon),
         )
 
     inner = (pl.ds(own_r, rows), pl.ds(own_c, cols))
@@ -116,11 +115,11 @@
         load.start()
     pl.semaphore_wait(barrier, 6)
     first = ahead(0, inputs, 0, 0, xtall, ext)
-    for turn in (1, 2, 0):
-        first[turn].start()
-    second = back(1, btall, 0, bext)
+    first[1].start()
+    first[2].start()
+    second = back(1, btall, bext)
     third = ahead(2, gskip, 0, 0, gtall, gext)
-    fourth = back(3, rext, back_c, rext)
+    fourth = back(3, rtall, rext)
 
     s_lat, s_lon = shift_lat[0], shift_lon[0]
     t_lat = jnp.clip(s_lat - li * (WLAT - halo_lat), 0, halo_lat)
@@ -143,58 +142,53 @@
     bias[0] = jnp.zeros((TOK, 2 * TOK), F32)
     bias[1] = jnp.concatenate([apart, apart], 1)
 
-    def attend(i, across, p):
-        at = p * 128
-        q = both(proj[i, :, pl.ds(at, 128)] * BF(0.125))
-        k = proj[i, :, pl.ds(FEAT + at, 128)]
-        v = proj[i, :, pl.ds(2 * FEAT + at, 128)]
+    def attend(i, u, across, p):
+        at, rr = p * 128, pl.ds(u * TOK, TOK)
+        q = both(proj[i, rr, pl.ds(at, 128)] * BF(0.125))
+        k = proj[i, rr, pl.ds(FEAT + at, 128)]
+        v = proj[i, rr, pl.ds(2 * FEAT + at, 128)]
         scores = dot_t(k, q) + bias[across]
         e = jnp.exp(scores - jnp.max(scores, 0, keepdims=True))
         w = (e * (1.0 / jnp.sum(e, 0, keepdims=True))).astype(BF)
-        soft[i, p] = w
-        mixed[:, pl.ds(at, 128)] = unite(t_dot(w, v)).astype(BF)
-
-    def attend_back(i, p):
-        at = p * 128
-        q = both(proj[i, :, pl.ds(at, 128)] * BF(0.125))
-        k = proj[i, :, pl.ds(FEAT + at, 128)]
-        v = proj[i, :, pl.ds(2 * FEAT + at, 128)]
-        g = both(mixed[:, pl.ds(at, 128)])
-        w = soft[i, p]
+        soft[i, u, p] = w
+        mixed[rr, pl.ds(at, 128)] = unite(t_dot(w, v)).astype(BF)
+
+    def attend_back(i, u, p):
+        at, rr = p * 128, pl.ds(pl.multiple_of(u * TOK, 16), TOK)
+        q = both(proj[i, rr, pl.ds(at, 128)] * BF(0.125))
+        k = proj[i, rr, pl.ds(FEAT + at, 128)]
+        v = proj[i, rr, pl.ds(2 * FEAT + at, 128)]
+        g = both(mixed[rr, pl.ds(at, 128)])
+        w = soft[i, u, p]
         dw = dot_t(v, g)
         wf = w.astype(F32)
         ds = (wf * (dw - jnp.sum(dw * wf, 0, keepdims=True))).astype(BF)
-        dproj[:, pl.ds(at, 128)] = (unite(t_dot(ds, k)) * 0.125).astype(BF)
-        dproj[:, pl.ds(FEAT + at, 128)] = dot(ds, q).astype(BF)
-        dproj[:, pl.ds(2 * FEAT + at, 128)] = dot(w, g).astype(BF)
+        dproj[rr, pl.ds(at, 128)] = (unite(t_dot(ds, k)) * 0.125).astype(BF)
+        dproj[rr, pl.ds(FEAT + at, 128)] = dot(ds, q).astype(BF)
+        dproj[rr, pl.ds(2 * FEAT + at, 128)] = dot(w, g).astype(BF)
 
     def windows(forward, ready, local_ref, tall, wide, results, copies):
         def step(i, carry):
-            across_lat, across_lon = ((i + 1) // 2) % 2, i // 2
-            wr = WLAT * (li + dlat * across_lat)
-            wc = WLON * (lj + dlon * across_lon)
+            across = (i, 1 - i)
+            wr = tuple(WLAT * (li + dlat * a) for a in across)
+            wc = WLON * (lj + dlon * i)
 
             @pl.when(i == 0)
             def _():
                 x = local_ref[pl.ds(s_lat, WLAT), pl.ds(s_lon, WLON)]
-                token[...] = x.reshape(TOK, FEAT)
+                token[pl.ds(0, TOK)] = x.reshape(TOK, FEAT)
+                ready[0].wait_recv()
+                x = tall[pl.ds(t_lat + wr[1], WLAT), pl.ds(s_lon, WLON)]
+                token[pl.ds(TOK, TOK)] = x.reshape(TOK, FEAT)
 
             @pl.when(i == 1)
             def _():
-                ready[0].wait_recv()
-                x = tall[pl.ds(t_lat + wr, WLAT), pl.ds(s_lon, WLON)]
-                token[...] = x.reshape(TOK, FEAT)
-
-            @pl.when(i == 2)
-            def _():
+                wide[pl.ds(halo_r, halo_lat), pl.ds(own_c, cols)] = tall[pl.ds(halo_r, halo_lat)]
                 ready[1].wait_recv()
                 ready[2].wait_recv()
-                wide[pl.ds(halo_r, halo_lat), pl.ds(own_c, cols)] = tall[pl.ds(halo_r, halo_lat)]
-
-            @pl.when(i >= 2)
-            def _():
-                x = wide[pl.ds(t_lat + wr, WLAT), pl.ds(t_lon + wc, WLON)]
-                token[...] = x.reshape(TOK, FEAT)
+                for u in range(2):
+                    x = wide[pl.ds(t_lat + wr[u], WLAT), pl.ds(t_lon + wc, WLON)]
+                    token[pl.ds(u * TOK, TOK)] = x.reshape(TOK, FEAT)
 
             if forward:
                 x = token[...].astype(F32)
@@ -203,48 +197,61 @@
                 inv = lax.rsqrt(jnp.mean(x * x, -1, keepdims=True) + EPS)
                 x = x * inv
                 norm[i] = x
-                rstd[i] = jnp.broadcast_to(inv, (TOK, 128))
+                rstd[i] = jnp.broadcast_to(inv, (2 * TOK, 128))
                 proj[i] = dot((x * gain_attn[...]).astype(BF), w_qkv[...]).astype(BF)
-                for p in range(PAIRS):
-                    attend(i, across_lat, p)
+                for u in range(2):
+                    for p in range(PAIRS):
+                        attend(i, u, across[u], p)
                 result = dot(mixed[...], w_out[...]).astype(BF)
             else:
                 mixed[...] = dot_t(token[...], w_out[...]).astype(BF)
-                for p in range(PAIRS):
-                    attend_back(i, p)
+
+                def back_rows(u, carry):
+                    for p in range(PAIRS):
+                        attend_back(i, u, p)
+                    return carry
+
+                lax.fori_loop(0, 2, back_rows, 0)
                 d = dot_t(dproj[...], w_qkv[...]).astype(BF).astype(F32) * gain_attn[...]
                 nn = norm[i]
                 inv = rstd[i][:, :1]
                 result = (inv * (
                     d - jnp.mean(d, -1, keepdims=True) - nn * jnp.mean(d * nn, -1, keepdims=True)
                 )).astype(BF)
-            result = result.reshape(WLAT, WLON, 2, FEAT)
-            for ref, at_c in results:
-                ref[pl.ds(back_r + wr, WLAT), pl.ds(at_c + wc, WLON)] = result
-            for turn, part in ((1, copies[:1]), (2, copies[1:4]), (3, copies[4:])):
-                @pl.when(i == turn)
-                def _(part=part):
-                    for copy in part:
-                        copy.start()
+            for u in range(2):
+                part = result[u * TOK:(u + 1) * TOK].reshape(WLAT, WLON, 2, FEAT)
+                for ref, at_c in results:
+                    ref[pl.ds(back_r + wr[u], WLAT), pl.ds(at_c + wc, WLON)] = part
+
+            @pl.when(i == 0)
+            def _():
+                copies[0].start()
+
+            @pl.when(i == 1)
+            def _():
+                for copy in copies[1:]:
+                    copy.start()
+
             return carry
 
-        lax.fori_loop(0, 4, step, 0)
+        lax.fori_loop(0, 2, step, 0)
 
     loads[0].wait()
     loads[1].wait()
     strip, slim = TOK // STRIPS, cols // STRIPS
     thin = slim // 2
 
-    def quarter_back(j, carry):
-        at = pl.multiple_of(j * FEAT, FEAT)
+    def part_back(j, carry):
+        at = pl.multiple_of(j * HALF, HALF)
         x = jnp.concatenate(
             [cot_coarse[:, k * thin:(k + 1) * thin].reshape(strip, 2 * FEAT) for k in range(STRIPS)], 0
         )
-        y = dot_t(x, w_merge[pl.ds(at, FEAT), :]).astype(BF)
-        gm[:, :, pl.ds(at, FEAT)] = y.reshape(STRIPS, strip, FEAT)
+        y = dot_t(x, w_merge[pl.ds(at, HALF), :]).astype(BF)
+        gm[:, :, pl.ds(at, HALF)] = y.reshape(STRIPS, strip, HALF)
         return carry
 
-    lax.fori_loop(0, 4, quarter_back, 0)
+    lax.fori_loop(0, 4 * FEAT // HALF, part_back, 0)
+    first[0].start()
     for load in loads[2:8]:
         load.wait()
     windows(True, first, own, xtall, ext, ((btall, 0), (bext, back_c)), second)
@@ -269,8 +276,8 @@
 
         @pl.when(turn == STRIPS - 1)
         def _():
-            for i in (1, 2, 4):
-                second[i].wait_recv()
+            second[1].wait_recv()
+            second[2].wait_recv()
             bext[pl.ds(bhalo_r, halo_lat), pl.ds(back_c, cols)] = btall[pl.ds(bhalo_r, halo_lat)]
             placed = bext[pl.ds(start_r, rows), pl.ds(start_c + slim * j, slim)]
             skip[:, mine] = (own[:, mine].astype(F32) + placed.astype(F32)).astype(BF)
@@ -298,43 +305,72 @@
         return carry
 
     lax.fori_loop(0, STRIPS, merge, 0)
-    for turn in (1, 2, 0):
-        third[turn].start()
-    gtall[pl.ds(own_r, rows)] = gskip[...]
-    gext[inner] = gskip[...]
+    third[1].start()
+    third[2].start()
+    spread = [
+        pltpu.make_async_copy(gskip, gtall.at[pl.ds(own_r, rows)], local_sem.at[10]),
+        pltpu.make_async_copy(gskip, gext.at[inner], local_sem.at[11]),
+    ]
+    for copy in spread:
+        copy.start()
     skip_out = pltpu.make_async_copy(skip, skip_hbm, out_sem.at[0])
     skip_out.start()
-    windows(False, third, gskip, gtall, gext, ((rext, back_c),), fourth)
 
     def coarse_part(j, carry):
-        at = pl.multiple_of(j * FEAT, FEAT)
+        @pl.when(j == 1)
+        def _():
+            third[0].start()
+
+        at = pl.multiple_of(j * HALF, HALF)
         x = merged.reshape(TOK, width)[...]
-        y = dot(x, w_merge[:, pl.ds(at, FEAT)]).astype(BF)
+        y = dot(x, w_merge[:, pl.ds(at, HALF)]).astype(BF)
         for k in range(STRIPS):
-            coarse[:, k * thin:(k + 1) * thin, :, pl.ds(at, FEAT)] = y[
+            coarse[:, k * thin:(k + 1) * thin, :, pl.ds(at, HALF)] = y[
                 k * strip:(k + 1) * strip
-            ].reshape(rows // 2, thin, 2, FEAT)
+            ].reshape(rows // 2, thin, 2, HALF)
         return carry
 
-    lax.fori_loop(0, 2, coarse_part, 0)
+    lax.fori_loop(0, 2 * FEAT // HALF, coarse_part, 0)
     coarse_out = pltpu.make_async_copy(coarse, coarse_hbm, out_sem.at[1])
     coarse_out.start()
-    for copy in fourth:
-        copy.wait_recv()
-
-    def finish(j, carry):
-        mine = pl.ds(4 * j, 4)
-        out[mine] = gskip[mine] + rext[pl.ds(start_r + 4 * j, 4), pl.ds(start_c, cols)]
+    for copy in spread:
+        copy.wait()
+    windows(False, third, gskip, gtall, gext, ((rtall, 0), (rext, back_c)), fourth)
+    fourth[0].wait_recv()
+    fourth[3].wait_recv()
+
+    def grad_out(turn):
+        j = turn if lj else lax.rem(turn + 1, STRIPS)
+        mine = pl.ds(slim * j, slim)
+        return pltpu.make_async_copy(out.at[:, mine], grad_hbm.at[:, mine], out_sem.at[2 + turn])
+
+    def finish(turn, carry):
+        j = turn if lj else lax.rem(turn + 1, STRIPS)
+        mine = pl.ds(slim * j, slim)
+
+        @pl.when(turn < STRIPS - 1)
+        def _():
+            placed = rtall[pl.ds(start_r, rows), pl.ds(start_c - back_c + slim * j, slim)]
+            out[:, mine] = gskip[:, mine] + placed
+
+        @pl.when(turn == STRIPS - 1)
+        def _():
+            rext[pl.ds(bhalo_r, halo_lat), pl.ds(back_c, cols)] = rtall[pl.ds(bhalo_r, halo_lat)]
+            fourth[1].wait_recv()
+            fourth[2].wait_recv()
+            placed = rext[pl.ds(start_r, rows), pl.ds(start_c + slim * j, slim)]
+            out[:, mine] = gskip[:, mine] + placed
+
+        grad_out(turn).start()
         return carry
 
-    lax.fori_loop(0, rows // 4, finish, 0)
-    grad_out = pltpu.make_async_copy(out, grad_hbm, out_sem.at[2])
-    grad_out.start()
+    lax.fori_loop(0, STRIPS, finish, 0)
     for copy in first + second + third + fourth:
         copy.wait_send()
     skip_out.wait()
     coarse_out.wait()
-    grad_out.wait()
+    for turn in range(STRIPS):
+        grad_out(turn).wait()
 
 
 def block(behind_lat, behind_lon, halo_lat, halo_lon, ident, args):
@@ -360,7 +396,7 @@
             pltpu.VMEM((1, feat), F32),
             pltpu.VMEM((1, 4 * feat), F32),
             tile,
-            tall, tall, tall,
+            tall, tall, tall, tall,
             pltpu.VMEM(wide, BF),
             pltpu.VMEM(wide, BF),
             pltpu.VMEM(wide, BF),
@@ -371,18 +407,18 @@
             pltpu.VMEM(w_merge.shape, BF),
             pltpu.VMEM((STRIPS, TOK // STRIPS, 4 * FEAT), BF),
             pltpu.VMEM((STRIPS, TOK // STRIPS, 4 * FEAT), BF),
-            pltpu.VMEM((TOK, FEAT), BF),
-            pltpu.VMEM((4, TOK, FEAT), F32),
-            pltpu.VMEM((4, TOK, 128), F32),
-            pltpu.VMEM((4, TOK, 3 * FEAT), BF),
-            pltpu.VMEM((TOK, FEAT), BF),
-            pltpu.VMEM((4, PAIRS, TOK, 2 * TOK), BF),
-            pltpu.VMEM((TOK, 3 * FEAT), BF),
+            pltpu.VMEM((2 * TOK, FEAT), BF),
+            pltpu.VMEM((2, 2 * TOK, FEAT), F32),
+            pltpu.VMEM((2, 2 * TOK, 128), F32),
+            pltpu.VMEM((2, 2 * TOK, 3 * FEAT), BF),
+            pltpu.VMEM((2 * TOK, FEAT), BF),
+            pltpu.VMEM((2, 2, PAIRS, TOK, 2 * TOK), BF),
+            pltpu.VMEM((2 * TOK, 3 * FEAT), BF),
             pltpu.VMEM((2, TOK, 2 * TOK), F32),
-            pltpu.SemaphoreType.DMA((10,)),
-            pltpu.SemaphoreType.DMA((3,)),
-            pltpu.SemaphoreType.DMA((4, 5)),
-            pltpu.SemaphoreType.DMA((4, 5)),
+            pltpu.SemaphoreType.DMA((12,)),
+            pltpu.SemaphoreType.DMA((2 + STRIPS,)),
+            pltpu.SemaphoreType.DMA((4, 4)),
+            pltpu.SemaphoreType.DMA((4, 4)),
         ],
         compiler_params=pltpu.CompilerParams(
             collective_id=ident, has_side_effects=True, vmem_limit_bytes=VMEM

time: 56.2 us -> 54.3 us (0.966)
  Pallas kernels: 53.7 us -> 51.3 us
    pallas_call x1, Pallas kernels: 52.6 us -> 50.2 us  [block(): pl.pallas_call(functools.partial(kernel, behind_lat, behind_lon, halo_lat...]
where the time goes in v2:
time: 54.3 us; the launch traced here: 54.2 us
  Pallas kernels  51.3 us (94%)
  between operations  2.16 us (4%)
  loops' own time  0.73 us (1%)
    pallas_call x1, Pallas kernels, block(): pl.pallas_call(functools.partial(kernel, behind_lat, behind_lon, halo_lat...  50.2 us
    pallas_call x1, Pallas kernels, hand_out(): pl.pallas_call(deliver, out_shape=tuple((jax.ShapeDtypeStruct(x.shape, x....  1.13 us

profile of v2, /device:TPU:1, one launch (start us, length us, event | category | flops | bytes accessed | tf_op | source)
XLA Modules:
  0.0 54.2 jit_solution(18388370602119428372)
XLA Ops:
  1.9 50.9 %conditional.1 = ((bf16[6,12,2,1024]{3,2,1,0:T(2,128)(2,1)S(1)}, bf16[12,24,2,512]{3,2,1,0:T(2,128)(2,1)S(1)}, bf16[12,24,2,512]{3,2,1,0:T(2,128)(2,1)S(1)})) conditional(s32[]{:T(128)} %bitcast.8, (f32[512]{0:T(512)}, f32[2048]{0:T(1024)}, s32[1]{0:T(128)}, s32[1]{0:T(128)}, bf16[12,24,2,512]{3,2,1,0:T(2,128)(2,1)}, ...), branch_computations={%region_0.0_spmd, %region_1.0_spmd, %region_2.0_spmd, %region_3.0_... | conditional | bytes 8 | solution.py:458
  2.1 50.2 %branch_1_fun.1 = (bf16[6,12,2,1024]{3,2,1,0:T(2,128)(2,1)S(1)}, bf16[12,24,2,512]{3,2,1,0:T(2,128)(2,1)S(1)}, bf16[12,24,2,512]{3,2,1,0:T(2,128)(2,1)S(1)}) custom-call(s32[1]{0:T(128)} %get-tuple-element.90.shift_lat, s32[1]{0:T(128)} %get-tuple-element.91.shift_lon, f32[1,512]{1,0:T(1,128)} %bitcast.14, f32[1,2048]{1,0:T(1,128)} %bitcast.10, ...), custom_call_target="tpu_custom_call" | custom-call | tf_op jit(solution)/shard_map/cond/branch_1_fun/pallas_call | solution.py:386
  52.8 1.1 %shard_map.121 = (bf16[6,12,2,1024]{3,2,1,0:T(2,128)(2,1)}, bf16[12,24,2,512]{3,2,1,0:T(2,128)(2,1)}, bf16[12,24,2,512]{3,2,1,0:T(2,128)(2,1)}) custom-call(bf16[6,12,2,1024]{3,2,1,0:T(2,128)(2,1)S(1)} %get-tuple-element.126.coarse, bf16[12,24,2,512]{3,2,1,0:T(2,128)(2,1)S(1)} %get-tuple-element.127.skip, bf16[12,24,2,512]{3,2,1,0:T(2,128)(2,1)S(1)} %get-tuple-element.128.grad), custom_call_target="tpu_custom_call" | custom-call | tf_op jit(solution)/shard_map/pallas_call | solution.py:445

commit v3 on v1

--- a/solution.py
+++ b/solution.py
@@ -38,7 +38,7 @@
     inputs, w_qkv_hbm, w_out_hbm, w_merge_hbm, cot_coarse_hbm, cot_skip_hbm,
     coarse_hbm, skip_hbm, grad_hbm,
     gain_attn, gain_merge,
-    own, xtall, btall, gtall, ext, bext, gext, rext, gskip, skip, cot_skip, cot_coarse, coarse, out,
+    own, xtall, btall, gtall, xflat, gflat, xquad, gquad, bext, rext, gskip, skip, cot_skip, cot_coarse, coarse, out,
     w_qkv, w_out, w_merge,
     gm, merged, token, norm, rstd, proj, mixed, soft, dproj, bias,
     local_sem, out_sem, send_sem, recv_sem,
@@ -72,12 +72,16 @@
             device_id_type=MESH,
         )
 
-    def ahead(phase, source, r, c, tall, wide):
-        er, ec = r + edge_r, c + edge_c
+    far_r, far_c = (1 - li) * WLAT, (1 - lj) * WLON
+    quad_r, quad_c = li * halo_lat, lj * halo_lon
+    qhalo_r, qhalo_c = (1 - li) * WLAT, (1 - lj) * WLON
+
+    def ahead(phase, source, tall, flat, quad):
+        er, ec = edge_r, edge_c
         return (
-            send(phase, 0, source, (er, c, halo_lat, cols), tall, (halo_r, 0), -dlat, 0),
-            send(phase, 1, source, (r, ec, rows, halo_lon), wide, (own_r, halo_c), 0, -dlon),
-            send(phase, 2, source, (er, ec, halo_lat, halo_lon), wide, (halo_r, halo_c), -dlat, -dlon),
+            send(phase, 0, source, (er, 0, halo_lat, cols), tall, (halo_r, 0), -dlat, 0),
+            send(phase, 1, source, (0, ec, rows, halo_lon), flat, (0, halo_c), 0, -dlon),
+            send(phase, 2, source, (er, ec, halo_lat, halo_lon), quad, (qhalo_r, qhalo_c), -dlat, -dlon),
         )
 
     def back(phase, tall, at_c, wide):
@@ -92,7 +96,6 @@
             send(phase, 4, wide, (near_r, ec, WLAT, halo_lon), wide, (near_r, bhalo_c), 0, dlon),
         )
 
-    inner = (pl.ds(own_r, rows), pl.ds(own_c, cols))
     loads = [
         pltpu.make_async_copy(src, dst, local_sem.at[i])
         for i, (src, dst) in enumerate((
@@ -103,7 +106,7 @@
             (w_qkv_hbm, w_qkv),
             (w_out_hbm, w_out),
             (inputs, xtall.at[pl.ds(own_r, rows)]),
-            (inputs, ext.at[inner]),
+            (inputs, xflat.at[:, pl.ds(own_c, cols)]),
             (cot_skip_hbm, cot_skip),
             (gain_merge_hbm, gain_merge),
         ))
@@ -115,11 +118,11 @@
     for load in loads:
         load.start()
     pl.semaphore_wait(barrier, 6)
-    first = ahead(0, inputs, 0, 0, xtall, ext)
-    for turn in (1, 2, 0):
-        first[turn].start()
+    first = ahead(0, inputs, xtall, xflat, xquad)
+    first[1].start()
+    first[0].start()
     second = back(1, btall, 0, bext)
-    third = ahead(2, gskip, 0, 0, gtall, gext)
+    third = ahead(2, gskip, gtall, gflat, gquad)
     fourth = back(3, rext, back_c, rext)
 
     s_lat, s_lon = shift_lat[0], shift_lon[0]
@@ -168,9 +171,9 @@
         dproj[:, pl.ds(FEAT + at, 128)] = dot(ds, q).astype(BF)
         dproj[:, pl.ds(2 * FEAT + at, 128)] = dot(w, g).astype(BF)
 
-    def windows(forward, ready, local_ref, tall, wide, results, copies):
+    def windows(forward, ready, local_ref, tall, flat, quad, results, copies):
         def step(i, carry):
-            across_lat, across_lon = ((i + 1) // 2) % 2, i // 2
+            across_lat, across_lon = i % 2, i // 2
             wr = WLAT * (li + dlat * across_lat)
             wc = WLON * (lj + dlon * across_lon)
 
@@ -188,12 +191,21 @@
             @pl.when(i == 2)
             def _():
                 ready[1].wait_recv()
+                x = flat[pl.ds(s_lat, WLAT), pl.ds(t_lon + wc, WLON)]
+                token[...] = x.reshape(TOK, FEAT)
+
+            @pl.when(i == 3)
+            def _():
+                mine = (pl.ds(quad_r, WLAT), pl.ds(quad_c, WLON))
+                quad[mine] = local_ref[pl.ds(far_r, WLAT), pl.ds(far_c, WLON)]
+                quad[pl.ds(qhalo_r, halo_lat), mine[1]] = tall[
+                    pl.ds(halo_r, halo_lat), pl.ds(far_c, WLON)
+                ]
+                quad[mine[0], pl.ds(qhalo_c, halo_lon)] = flat[
+                    pl.ds(far_r, WLAT), pl.ds(halo_c, halo_lon)
+                ]
                 ready[2].wait_recv()
-                wide[pl.ds(halo_r, halo_lat), pl.ds(own_c, cols)] = tall[pl.ds(halo_r, halo_lat)]
-
-            @pl.when(i >= 2)
-            def _():
-                x = wide[pl.ds(t_lat + wr, WLAT), pl.ds(t_lon + wc, WLON)]
+                x = quad[pl.ds(t_lat, WLAT), pl.ds(t_lon, WLON)]
                 token[...] = x.reshape(TOK, FEAT)
 
             if forward:
@@ -221,7 +233,7 @@
             result = result.reshape(WLAT, WLON, 2, FEAT)
             for ref, at_c in results:
                 ref[pl.ds(back_r + wr, WLAT), pl.ds(at_c + wc, WLON)] = result
-            for turn, part in ((1, copies[:1]), (2, copies[1:4]), (3, copies[4:])):
+            for turn, part in ((1, copies[:1]), (2, copies[4:]), (3, copies[1:4])):
                 @pl.when(i == turn)
                 def _(part=part):
                     for copy in part:
@@ -245,9 +257,10 @@
         return carry
 
     lax.fori_loop(0, 4, quarter_back, 0)
+    first[2].start()
     for load in loads[2:8]:
         load.wait()
-    windows(True, first, own, xtall, ext, ((btall, 0), (bext, back_c)), second)
+    windows(True, first, own, xtall, xflat, xquad, ((btall, 0), (bext, back_c)), second)
     loads[8].wait()
     loads[9].wait()
     second[0].wait_recv()
@@ -298,14 +311,12 @@
         return carry
 
     lax.fori_loop(0, STRIPS, merge, 0)
-    for turn in (1, 2, 0):
-        third[turn].start()
+    third[1].start()
+    third[0].start()
     gtall[pl.ds(own_r, rows)] = gskip[...]
-    gext[inner] = gskip[...]
+    gflat[:, pl.ds(own_c, cols)] = gskip[...]
     skip_out = pltpu.make_async_copy(skip, skip_hbm, out_sem.at[0])
     skip_out.start()
-    windows(False, third, gskip, gtall, gext, ((rext, back_c),), fourth)
-
     def coarse_part(j, carry):
         at = pl.multiple_of(j * FEAT, FEAT)
         x = merged.reshape(TOK, width)[...]
@@ -319,6 +330,8 @@
     lax.fori_loop(0, 2, coarse_part, 0)
     coarse_out = pltpu.make_async_copy(coarse, coarse_hbm, out_sem.at[1])
     coarse_out.start()
+    third[2].start()
+    windows(False, third, gskip, gtall, gflat, gquad, ((rext, back_c),), fourth)
     for copy in fourth:
         copy.wait_recv()
 
@@ -347,6 +360,8 @@
     anyw = pl.BlockSpec(memory_space=pl.ANY)
     tile, coarse = pltpu.VMEM(inputs.shape, BF), pltpu.VMEM(cot_coarse.shape, BF)
     tall = pltpu.VMEM((rows + halo_lat, cols, lev, feat), BF)
+    flat = pltpu.VMEM((rows, cols + halo_lon, lev, feat), BF)
+    quad = pltpu.VMEM((WLAT + halo_lat, WLON + halo_lon, lev, feat), BF)
     return pl.pallas_call(
         functools.partial(kernel, behind_lat, behind_lon, halo_lat, halo_lon),
         out_shape=(
@@ -360,9 +375,7 @@
             pltpu.VMEM((1, feat), F32),
             pltpu.VMEM((1, 4 * feat), F32),
             tile,
-            tall, tall, tall,
-            pltpu.VMEM(wide, BF),
-            pltpu.VMEM(wide, BF),
+            tall, tall, tall, flat, flat, quad, quad,
             pltpu.VMEM(wide, BF),
             pltpu.VMEM(wide, BF),
             tile, tile, tile, coarse, coarse, tile,

time: 56.2 us -> 54.9 us (0.977)
  Pallas kernels: 53.7 us -> 52.3 us
    pallas_call x1, Pallas kernels: 52.6 us -> 51.1 us  [block(): pl.pallas_call(functools.partial(kernel, behind_lat, behind_lon, halo_lat...]
where the time goes in v3:
time: 54.9 us; the launch traced here: 54.8 us
  Pallas kernels  52.3 us (95%)
  between operations  2.12 us (4%)
    pallas_call x1, Pallas kernels, block(): pl.pallas_call(functools.partial(kernel, behind_lat, behind_lon, halo_lat...  51.1 us
    pallas_call x1, Pallas kernels, hand_out(): pl.pallas_call(deliver, out_shape=tuple((jax.ShapeDtypeStruct(x.shape, x....  1.13 us

profile of v3, /device:TPU:1, one launch (start us, length us, event | category | flops | bytes accessed | tf_op | source)
XLA Modules:
  0.0 54.8 jit_solution(1917742885462844674)
XLA Ops:
  1.9 51.6 %conditional.1 = ((bf16[6,12,2,1024]{3,2,1,0:T(2,128)(2,1)S(1)}, bf16[12,24,2,512]{3,2,1,0:T(2,128)(2,1)S(1)}, bf16[12,24,2,512]{3,2,1,0:T(2,128)(2,1)S(1)})) conditional(s32[]{:T(128)} %bitcast.8, (f32[512]{0:T(512)}, f32[2048]{0:T(1024)}, s32[1]{0:T(128)}, s32[1]{0:T(128)}, bf16[12,24,2,512]{3,2,1,0:T(2,128)(2,1)}, ...), branch_computations={%region_0.0_spmd, %region_1.0_spmd, %region_2.0_spmd, %region_3.0_... | conditional | bytes 8 | solution.py:435
  2.1 51.1 %branch_2_fun.1 = (bf16[6,12,2,1024]{3,2,1,0:T(2,128)(2,1)S(1)}, bf16[12,24,2,512]{3,2,1,0:T(2,128)(2,1)S(1)}, bf16[12,24,2,512]{3,2,1,0:T(2,128)(2,1)S(1)}) custom-call(s32[1]{0:T(128)} %get-tuple-element.100.shift_lat, s32[1]{0:T(128)} %get-tuple-element.101.shift_lon, f32[1,512]{1,0:T(1,128)} %bitcast.15, f32[1,2048]{1,0:T(1,128)} %bitcast.11, ...), custom_call_target="tpu_custom_call" | custom-call | tf_op jit(solution)/shard_map/cond/branch_2_fun/pallas_call | solution.py:365
  53.5 1.1 %shard_map.121 = (bf16[6,12,2,1024]{3,2,1,0:T(2,128)(2,1)}, bf16[12,24,2,512]{3,2,1,0:T(2,128)(2,1)}, bf16[12,24,2,512]{3,2,1,0:T(2,128)(2,1)}) custom-call(bf16[6,12,2,1024]{3,2,1,0:T(2,128)(2,1)S(1)} %get-tuple-element.126.coarse, bf16[12,24,2,512]{3,2,1,0:T(2,128)(2,1)S(1)} %get-tuple-element.127.skip, bf16[12,24,2,512]{3,2,1,0:T(2,128)(2,1)S(1)} %get-tuple-element.128.grad), custom_call_target="tpu_custom_call" | custom-call | tf_op jit(solution)/shard_map/pallas_call | solution.py:422

commit v4 on v3

--- a/solution.py
+++ b/solution.py
@@ -34,10 +34,10 @@
 
 def kernel(
     behind_lat, behind_lon, halo_lat, halo_lon,
-    shift_lat, shift_lon, gain_attn_hbm, gain_merge_hbm,
+    shift_lat_hbm, shift_lon, gain_attn_hbm, gain_merge_hbm,
     inputs, w_qkv_hbm, w_out_hbm, w_merge_hbm, cot_coarse_hbm, cot_skip_hbm,
     coarse_hbm, skip_hbm, grad_hbm,
-    gain_attn, gain_merge,
+    shift_lat, gain_attn, gain_merge,
     own, xtall, btall, gtall, xflat, gflat, xquad, gquad, bext, rext, gskip, skip, cot_skip, cot_coarse, coarse, out,
     w_qkv, w_out, w_merge,
     gm, merged, token, norm, rstd, proj, mixed, soft, dproj, bias,
@@ -109,6 +109,7 @@
             (inputs, xflat.at[:, pl.ds(own_c, cols)]),
             (cot_skip_hbm, cot_skip),
             (gain_merge_hbm, gain_merge),
+            (shift_lat_hbm, shift_lat),
         ))
     ]
     barrier = pltpu.get_barrier_semaphore()
@@ -125,6 +126,7 @@
     third = ahead(2, gskip, gtall, gflat, gquad)
     fourth = back(3, rext, back_c, rext)
 
+    loads[10].wait()
     s_lat, s_lon = shift_lat[0], shift_lon[0]
     t_lat = jnp.clip(s_lat - li * (WLAT - halo_lat), 0, halo_lat)
     t_lon = jnp.clip(s_lon - lj * (WLON - halo_lon), 0, halo_lon)
@@ -369,9 +371,10 @@
             jax.ShapeDtypeStruct(inputs.shape, BF),
             jax.ShapeDtypeStruct(inputs.shape, BF),
         ),
-        in_specs=[smem, smem] + [hbm] * 8,
+        in_specs=[hbm, smem] + [hbm] * 8,
         out_specs=(anyw, anyw, anyw),
         scratch_shapes=[
+            pltpu.SMEM((1,), jnp.int32),
             pltpu.VMEM((1, feat), F32),
             pltpu.VMEM((1, 4 * feat), F32),
             tile,
@@ -392,7 +395,7 @@
             pltpu.VMEM((4, PAIRS, TOK, 2 * TOK), BF),
             pltpu.VMEM((TOK, 3 * FEAT), BF),
             pltpu.VMEM((2, TOK, 2 * TOK), F32),
-            pltpu.SemaphoreType.DMA((10,)),
+            pltpu.SemaphoreType.DMA((11,)),
             pltpu.SemaphoreType.DMA((3,)),
             pltpu.SemaphoreType.DMA((4, 5)),
             pltpu.SemaphoreType.DMA((4, 5)),
@@ -429,13 +432,14 @@
 
 
 def local(*args):
-    half_lat, half_lon = WLAT // 2, WLON // 2
-    behind_lat = (args[1][0] > half_lat).astype(jnp.int32)
-    behind_lon = (args[2][0] > half_lon).astype(jnp.int32)
+    half = WLON // 2
+    shift = args[2][0]
+    behind = (shift > half).astype(jnp.int32)
+    narrow = (jnp.minimum(shift, WLON - shift) <= half // 2).astype(jnp.int32)
     results = lax.switch(
-        2 * behind_lat + behind_lon,
+        2 * narrow + behind,
         [
-            functools.partial(block, bool(i // 2), bool(i % 2), half_lat, half_lon, i)
+            functools.partial(block, False, bool(i % 2), WLAT - 1, half // (1 + i // 2), i)
             for i in range(4)
         ],
         args,

time: 54.9 us -> 56 us (1.020)
  the two profiles are of different devices: /device:TPU:1 before, /device:TPU:24 now
where the time goes in v4:
time: 56 us; the launch traced here: 55.8 us
  Pallas kernels  54.1 us (97%)
  between operations  1.48 us (3%)
    pallas_call x1, Pallas kernels, block(): pl.pallas_call(functools.partial(kernel, behind_lat, behind_lon, halo_lat...  53 us
    pallas_call x1, Pallas kernels, hand_out(): pl.pallas_call(deliver, out_shape=tuple((jax.ShapeDtypeStruct(x.shape, x....  1.13 us

profile of v4, /device:TPU:24, one launch (start us, length us, event | category | flops | bytes accessed | tf_op | source)
XLA Modules:
  0.0 55.8 jit_solution(8439136239832955312)
XLA Ops:
  1.3 53.2 %conditional.1 = ((bf16[6,12,2,1024]{3,2,1,0:T(2,128)(2,1)S(1)}, bf16[12,24,2,512]{3,2,1,0:T(2,128)(2,1)S(1)}, bf16[12,24,2,512]{3,2,1,0:T(2,128)(2,1)S(1)})) conditional(s32[]{:T(128)} %clamp.3, (f32[512]{0:T(512)}, f32[2048]{0:T(1024)}, s32[1]{0:T(128)}, s32[1]{0:T(128)}, bf16[12,24,2,512]{3,2,1,0:T(2,128)(2,1)}, ...), branch_computations={%region_0.0_spmd, %region_1.0_spmd, %region_2.0_spmd, %region_3.0_... | conditional | bytes 8 | solution.py:439
  1.3 53.0 %branch_1_fun.1 = (bf16[6,12,2,1024]{3,2,1,0:T(2,128)(2,1)S(1)}, bf16[12,24,2,512]{3,2,1,0:T(2,128)(2,1)S(1)}, bf16[12,24,2,512]{3,2,1,0:T(2,128)(2,1)S(1)}) custom-call(s32[1]{0:T(128)} %get-tuple-element.90.shift_lat_hbm, s32[1]{0:T(128)} %get-tuple-element.91.shift_lon, f32[1,512]{1,0:T(1,128)} %bitcast.17, f32[1,2048]{1,0:T(1,128)} %bitcast.13, ...), custom_call_target="tpu_custom_call" | custom-call | tf_op jit(solution)/shard_map/cond/branch_1_fun/pallas_call | solution.py:367
  54.5 1.1 %shard_map.121 = (bf16[6,12,2,1024]{3,2,1,0:T(2,128)(2,1)}, bf16[12,24,2,512]{3,2,1,0:T(2,128)(2,1)}, bf16[12,24,2,512]{3,2,1,0:T(2,128)(2,1)}) custom-call(bf16[6,12,2,1024]{3,2,1,0:T(2,128)(2,1)S(1)} %get-tuple-element.126.coarse, bf16[12,24,2,512]{3,2,1,0:T(2,128)(2,1)S(1)} %get-tuple-element.127.skip, bf16[12,24,2,512]{3,2,1,0:T(2,128)(2,1)S(1)} %get-tuple-element.128.grad), custom_call_target="tpu_custom_call" | custom-call | tf_op jit(solution)/shard_map/pallas_call | solution.py:425

commit v5 on v4

--- a/solution.py
+++ b/solution.py
@@ -156,22 +156,32 @@
         scores = dot_t(k, q) + bias[across]
         e = jnp.exp(scores - jnp.max(scores, 0, keepdims=True))
         w = (e * (1.0 / jnp.sum(e, 0, keepdims=True))).astype(BF)
-        soft[i, p] = w
+        soft[i, p // 2, :, pl.ds(p % 2 * 2 * TOK, 2 * TOK)] = w
         mixed[:, pl.ds(at, 128)] = unite(t_dot(w, v)).astype(BF)
 
+    head_of = lax.broadcasted_iota(jnp.int32, (TOK, 256), 1) // 64
+    zeros = jnp.zeros((TOK, 256), BF)
+
+    def four(x):
+        return jnp.concatenate([jnp.where(head_of == h, x, zeros) for h in range(4)], 0)
+
     def attend_back(i, p):
-        at = p * 128
-        q = both(proj[i, :, pl.ds(at, 128)] * BF(0.125))
-        k = proj[i, :, pl.ds(FEAT + at, 128)]
-        v = proj[i, :, pl.ds(2 * FEAT + at, 128)]
-        g = both(mixed[:, pl.ds(at, 128)])
+        at = p * 256
+        q = four(proj[i, :, pl.ds(at, 256)] * BF(0.125))
+        k = proj[i, :, pl.ds(FEAT + at, 256)]
+        v = proj[i, :, pl.ds(2 * FEAT + at, 256)]
+        g = four(mixed[:, pl.ds(at, 256)])
         w = soft[i, p]
         dw = dot_t(v, g)
         wf = w.astype(F32)
         ds = (wf * (dw - jnp.sum(dw * wf, 0, keepdims=True))).astype(BF)
-        dproj[:, pl.ds(at, 128)] = (unite(t_dot(ds, k)) * 0.125).astype(BF)
-        dproj[:, pl.ds(FEAT + at, 128)] = dot(ds, q).astype(BF)
-        dproj[:, pl.ds(2 * FEAT + at, 128)] = dot(w, g).astype(BF)
+        d = t_dot(ds, k)
+        dq = d[:TOK]
+        for h in range(1, 4):
+            dq = jnp.where(head_of == h, d[h * TOK:(h + 1) * TOK], dq)
+        dproj[:, pl.ds(at, 256)] = (dq * 0.125).astype(BF)
+        dproj[:, pl.ds(FEAT + at, 256)] = dot(ds, q).astype(BF)
+        dproj[:, pl.ds(2 * FEAT + at, 256)] = dot(w, g).astype(BF)
 
     def windows(forward, ready, local_ref, tall, flat, quad, results, copies):
         def step(i, carry):
@@ -224,7 +234,7 @@
                 result = dot(mixed[...], w_out[...]).astype(BF)
             else:
                 mixed[...] = dot_t(token[...], w_out[...]).astype(BF)
-                for p in range(PAIRS):
+                for p in range(PAIRS // 2):
                     attend_back(i, p)
                 d = dot_t(dproj[...], w_qkv[...]).astype(BF).astype(F32) * gain_attn[...]
                 nn = norm[i]
@@ -337,19 +347,23 @@
     for copy in fourth:
         copy.wait_recv()
 
+    def grad_out(j):
+        mine = pl.ds(4 * j, 4)
+        return pltpu.make_async_copy(out.at[mine], grad_hbm.at[mine], out_sem.at[2 + j])
+
     def finish(j, carry):
         mine = pl.ds(4 * j, 4)
         out[mine] = gskip[mine] + rext[pl.ds(start_r + 4 * j, 4), pl.ds(start_c, cols)]
+        grad_out(j).start()
         return carry
 
     lax.fori_loop(0, rows // 4, finish, 0)
-    grad_out = pltpu.make_async_copy(out, grad_hbm, out_sem.at[2])
-    grad_out.start()
     for copy in first + second + third + fourth:
         copy.wait_send()
     skip_out.wait()
     coarse_out.wait()
-    grad_out.wait()
+    for j in range(rows // 4):
+        grad_out(j).wait()
 
 
 def block(behind_lat, behind_lon, halo_lat, halo_lon, ident, args):
@@ -392,11 +406,11 @@
             pltpu.VMEM((4, TOK, 128), F32),
             pltpu.VMEM((4, TOK, 3 * FEAT), BF),
             pltpu.VMEM((TOK, FEAT), BF),
-            pltpu.VMEM((4, PAIRS, TOK, 2 * TOK), BF),
+            pltpu.VMEM((4, PAIRS // 2, TOK, 4 * TOK), BF),
             pltpu.VMEM((TOK, 3 * FEAT), BF),
             pltpu.VMEM((2, TOK, 2 * TOK), F32),
             pltpu.SemaphoreType.DMA((11,)),
-            pltpu.SemaphoreType.DMA((3,)),
+            pltpu.SemaphoreType.DMA((2 + rows // 4,)),
             pltpu.SemaphoreType.DMA((4, 5)),
             pltpu.SemaphoreType.DMA((4, 5)),
         ],

time: 56 us -> 50.9 us (0.909)
  the two profiles are of different devices: /device:TPU:24 before, /device:TPU:1 now
where the time goes in v5:
time: 50.9 us; the launch traced here: 50.8 us
  Pallas kernels  48.9 us (96%)
  between operations  1.48 us (3%)
    pallas_call x1, Pallas kernels, block(): pl.pallas_call(functools.partial(kernel, behind_lat, behind_lon, halo_lat...  47.7 us
    pallas_call x1, Pallas kernels, hand_out(): pl.pallas_call(deliver, out_shape=tuple((jax.ShapeDtypeStruct(x.shape, x....  1.13 us

profile of v5, /device:TPU:1, one launch (start us, length us, event | category | flops | bytes accessed | tf_op | source)
XLA Modules:
  0.0 50.8 jit_solution(14671962687646357198)
XLA Ops:
  1.3 48.2 %conditional.1 = ((bf16[6,12,2,1024]{3,2,1,0:T(2,128)(2,1)S(1)}, bf16[12,24,2,512]{3,2,1,0:T(2,128)(2,1)S(1)}, bf16[12,24,2,512]{3,2,1,0:T(2,128)(2,1)S(1)})) conditional(s32[]{:T(128)} %clamp.3, (f32[512]{0:T(512)}, f32[2048]{0:T(1024)}, s32[1]{0:T(128)}, s32[1]{0:T(128)}, bf16[12,24,2,512]{3,2,1,0:T(2,128)(2,1)}, ...), branch_computations={%region_0.0_spmd, %region_1.0_spmd, %region_2.0_spmd, %region_3.0_... | conditional | bytes 8 | solution.py:453
  1.5 47.7 %branch_2_fun.1 = (bf16[6,12,2,1024]{3,2,1,0:T(2,128)(2,1)S(1)}, bf16[12,24,2,512]{3,2,1,0:T(2,128)(2,1)S(1)}, bf16[12,24,2,512]{3,2,1,0:T(2,128)(2,1)S(1)}) custom-call(s32[1]{0:T(128)} %get-tuple-element.100.shift_lat_hbm, s32[1]{0:T(128)} %get-tuple-element.101.shift_lon, f32[1,512]{1,0:T(1,128)} %bitcast.18, f32[1,2048]{1,0:T(1,128)} %bitcast.14, ...), custom_call_target="tpu_custom_call" | custom-call | tf_op jit(solution)/shard_map/cond/branch_2_fun/pallas_call | solution.py:381
  49.5 1.1 %shard_map.121 = (bf16[6,12,2,1024]{3,2,1,0:T(2,128)(2,1)}, bf16[12,24,2,512]{3,2,1,0:T(2,128)(2,1)}, bf16[12,24,2,512]{3,2,1,0:T(2,128)(2,1)}) custom-call(bf16[6,12,2,1024]{3,2,1,0:T(2,128)(2,1)S(1)} %get-tuple-element.126.coarse, bf16[12,24,2,512]{3,2,1,0:T(2,128)(2,1)S(1)} %get-tuple-element.127.skip, bf16[12,24,2,512]{3,2,1,0:T(2,128)(2,1)S(1)} %get-tuple-element.128.grad), custom_call_target="tpu_custom_call" | custom-call | tf_op jit(solution)/shard_map/pallas_call | solution.py:439
